TPU v7x, 128 devices: a whole 4x4x4 slice. The times are simulated.
128 devices in a mesh: seq: 64 (over z_lo, y, x, core), grp: 2 (over z_hi).
Axes of the slice: x: 4, y: 4, z: 4 (z_hi: 2, z_lo: 2; z = z_hi * 2 + z_lo), core: 2. Of those that a mesh axis runs over, the one named last changes fastest.
Arguments:
- inputs: bfloat16 [8192, 2048], P('seq'), may hold values from -16 to 16
- attention_gain: float32 [2048], replicated, may hold values from 0.25 to 1.75
- query_weight: bfloat16 [2048, 2048], P('seq', 'grp'), may hold values from -0.125 to 0.125
- key_matrix: bfloat16 [2048, 1024], P('seq', 'grp'), may hold values from -0.125 to 0.125
- value_matrix: bfloat16 [2048, 1024], P('seq', 'grp'), may hold values from -0.125 to 0.125
- gate_weight: bfloat16 [2048, 16], P('seq', 'grp'), may hold values from -0.125 to 0.125
- query_gain: float32 [128], replicated, may hold values from 0.25 to 1.75
- key_gain: float32 [128], replicated, may hold values from 0.25 to 1.75
- out_weight: bfloat16 [2048, 2048], P('grp', 'seq'), may hold values from -3 to 3
- feed_gain: float32 [2048], replicated, may hold values from 0.25 to 1.75
- feed_gate: bfloat16 [2048, 6144], P('seq', 'grp'), may hold values from -0.125 to 0.125
- feed_up: bfloat16 [2048, 6144], P('seq', 'grp'), may hold values from -0.125 to 0.125
- feed_down: bfloat16 [6144, 2048], P('grp', 'seq'), may hold values from -0.078125 to 0.078125
- cotangent: bfloat16 [8192, 2048], P('seq'), may hold values from -16 to 16
Outputs:
- output: bfloat16 [8192, 2048], P('seq')
- grad_inputs: bfloat16 [8192, 2048], P('seq')
- grad_attention_gain: float32 [2048], P('seq')
- grad_query_weight: float32 [2048, 2048], P('seq', 'grp')
- grad_key_weight: float32 [2048, 1024], P('seq', 'grp')
- grad_value_weight: float32 [2048, 1024], P('seq', 'grp')
- grad_gate_weight: float32 [2048, 16], P('seq', 'grp')
- grad_query_gain: float32 [128], replicated
- grad_key_gain: float32 [128], replicated
- grad_out_weight: float32 [2048, 2048], P('grp', 'seq')
- grad_feed_gain: float32 [2048], P('seq')
- grad_feed_gate: float32 [2048, 6144], P('seq', 'grp')
- grad_feed_up: float32 [2048, 6144], P('seq', 'grp')
- grad_feed_down: float32 [6144, 2048], P('grp', 'seq')
All inputs are finite; a program needn't handle non-finite values.
Results may differ from a plain program's by a relative error of at most 0.022.
Values may be sent and summed in bfloat16 or wider, within the bound.
A program may use at most 256 MiB of HBM per device.

v0:
```python
from types import SimpleNamespace

import jax
import jax.numpy as jnp
import numpy as np
from jax import lax
from jax.experimental import pallas as pl
from jax.experimental.pallas import tpu as pltpu
from jax.sharding import PartitionSpec as P

EPSILON = 1e-06
ROPE_BASE = 1000000.0
WIDTH = 2048
HEAD = 128
EIGHTH = 768
ATT = 896
PROJ = 512
SCALE = HEAD**-0.5
LOG2E = 1.4426950408889634
LN2 = 0.6931471805599453
BF, F32 = jnp.bfloat16, jnp.float32
MESH = pl.DeviceIdType.MESH
ALL = slice(None)


def mm(a, b):
    return jnp.dot(a, b, preferred_element_type=F32)


def mm_tb(a, b):
    return lax.dot_general(a, b, (((1,), (1,)), ((), ())), preferred_element_type=F32)


def rms_scale(v):
    return lax.rsqrt(jnp.mean(v * v, axis=-1, keepdims=True) + EPSILON)


def rms_back(v, gain, dy):
    r = rms_scale(v)
    u = gain * dy
    dv = r * (u - v * (r * r * jnp.mean(u * v, axis=-1, keepdims=True)))
    return dv, jnp.sum(dy * v * r, axis=0, keepdims=True)


def rope(v, cos, sin):
    return v * cos + pltpu.roll(v, HEAD // 2, 1) * sin


def rope_back(v, cos, sin):
    return v * cos + pltpu.roll(v * sin, HEAD // 2, 1)


def three_parts(v, lanes):
    hi = v.astype(BF).astype(F32)
    mid = (v - hi).astype(BF).astype(F32)
    low = v - hi - mid
    return jnp.where(
        lanes == 0, hi, jnp.where(lanes == 1, mid, jnp.where(lanes == 2, low, 0.0))
    ).astype(BF)


def select(row_of, shape):
    row = lax.broadcasted_iota(jnp.int32, shape, 0)
    col = lax.broadcasted_iota(jnp.int32, shape, 1)
    return jnp.where(row_of(row, col), 1.0, 0.0).astype(BF)


def body(R):
    s, zh = lax.axis_index("seq"), lax.axis_index("grp")
    c = lax.rem(s, 2)
    x = lax.rem(lax.div(s, 2), 4)
    y = lax.rem(lax.div(s, 8), 4)
    zl = lax.div(s, 32)
    z = zh * 2 + zl
    j = y * 4 + x
    me = zl * 2 + c

    def up(v, k):
        return lax.rem(v + k, 4)

    def dev(zz, yy, xx, cc):
        return (lax.rem(zz, 2) * 32 + yy * 8 + xx * 2 + cc, lax.div(zz, 2))

    sib = dev(z, y, x, 1 - c)
    zs = [up(z, 1), up(z, 3), up(z, 2)]
    zdev = [dev(v, y, x, c) for v in zs]
    part = (zl_dev := (1 - zl) * 32 + y * 8 + x * 2 + c, zh)
    diag = ((1 - zl) * 32 + y * 8 + x * 2 + 1 - c, zh)
    other = (zl_dev, 1 - zh)
    xdev = [dev(z, y, up(x, k), c) for k in (1, 3, 2)]
    ydev = [dev(z, up(y, k), x, c) for k in (1, 3, 2)]

    barrier = pltpu.get_barrier_semaphore()
    zsib = [dev(v, y, x, 1 - c) for v in zs]
    greet = [sib] + zdev + zsib + xdev + ydev
    for d in greet:
        pl.semaphore_signal(barrier, inc=1, device_id=d, device_id_type=MESH)

    count = [0]

    def ids(k):
        count[0] += k
        return count[0] - k

    class Group:
        def __init__(self, k, base=None):
            self.base, self.sent = ids(k) if base is None else base, []

        def copy(self, src, dst, d, i):
            i += self.base
            return pltpu.make_async_remote_copy(
                src_ref=src, dst_ref=dst, send_sem=R.send.at[i], recv_sem=R.recv.at[i],
                device_id=d, device_id_type=MESH,
            )

        def run(self, ends, d, i):
            self.copy(*ends(), d, i).start()
            self.sent.append(lambda: self.copy(*ends(), d, i))

        def go(self, src, dst, d, i):
            self.run(lambda: (src, dst), d, i)

        def got(self, ref, i):
            self.copy(ref, ref, sib, i).wait_recv()

        def end(self):
            for cp in self.sent:
                cp().wait_send()

    def exchange(buf, wl, base, cs=ALL):
        g = Group(3, base)

        def start():
            buf[zl, y, x, c, :, cs] = wl[me, :, cs]
            dst = buf.at[zl, y, x, c, :, cs]
            g.go(wl.at[zl * 2 + 1 - c, :, cs], dst, sib, 0)
            g.go(wl.at[(1 - zl) * 2 + c, :, cs], dst, part, 1)
            g.go(wl.at[(1 - zl) * 2 + 1 - c, :, cs], dst, diag, 2)

        def wait():
            g.got(buf.at[zl, y, x, 1 - c, :, cs], 0)
            g.got(buf.at[1 - zl, y, x, c, :, cs], 1)
            g.got(buf.at[1 - zl, y, x, 1 - c, :, cs], 2)

        return start, wait, g.end

    def give_back(src, dst, base):
        g = Group(3, base)

        def start():
            dst[me] = src[zl, y, x, c]
            g.go(src.at[zl, y, x, 1 - c], dst.at[me], sib, 0)
            g.go(src.at[1 - zl, y, x, c], dst.at[me], part, 1)
            g.go(src.at[1 - zl, y, x, 1 - c], dst.at[me], diag, 2)

        def wait():
            g.got(dst.at[zl * 2 + 1 - c], 0)
            g.got(dst.at[(1 - zl) * 2 + c], 1)
            g.got(dst.at[(1 - zl) * 2 + 1 - c], 2)

        return start, wait, g.end

    a_y = SimpleNamespace(
        full=lambda p: (0, p), half=lambda p, h: (0, p, ALL, h), elem=lambda p, k, h: (0, p, k, h),
        k=4, pos=y, dev=ydev,
    )
    a_x = SimpleNamespace(
        full=lambda p: (0, y, p), half=lambda p, h: (0, y, p, h), elem=lambda p, k, h: (0, y, p, h),
        k=1, pos=x, dev=xdev,
    )
    b_x = SimpleNamespace(
        full=lambda p: (1, ALL, p), half=lambda p, h: (1, ALL, p, h), elem=lambda p, k, h: (1, k, p, h),
        k=4, pos=x, dev=xdev,
    )
    b_y = SimpleNamespace(
        full=lambda p: (1, p, x), half=lambda p, h: (1, p, x, h), elem=lambda p, k, h: (1, p, x, h),
        k=1, pos=y, dev=ydev,
    )

    def gather_ring(buf, a, cs, base):
        g, p = Group(6, base), a.pos
        left, right, across = up(p, 3), up(p, 1), up(p, 2)

        def half(q, h):
            at = a.half(q, h)
            return buf.at[at if cs is None else at + (ALL,) * (5 - len(at)) + (cs,)]

        def s1():
            for i, (h, d) in enumerate(((0, 0), (1, 1), (1, 0), (0, 1))):
                g.run(lambda h=h: (half(p, h), half(p, h)), a.dev[d], i)

        def s2():
            g.got(half(left, 0), 0)
            g.run(lambda: (half(left, 0), half(left, 0)), a.dev[0], 4)
            g.got(half(right, 1), 1)
            g.run(lambda: (half(right, 1), half(right, 1)), a.dev[1], 5)

        def s3():
            g.got(half(left, 1), 2)
            g.got(half(right, 0), 3)

        def s4():
            g.got(half(across, 0), 4)
            g.got(half(across, 1), 5)

        return s1, s2, s3, s4, g.end

    def gather(buf, base, cs=None):
        one = [gather_ring(buf, a_x, cs, base), gather_ring(buf, b_y, cs, base + 6)]
        two = [gather_ring(buf, a_y, cs, base + 12), gather_ring(buf, b_x, cs, base + 18)]

        def t1():
            for r in one:
                r[0]()

        def t2():
            for r in one:
                r[1]()

        def t3():
            for r, q in zip(one, two):
                r[2]()
                r[3]()
                q[0]()

        def t4():
            for r in two:
                r[1]()

        def t5():
            for r in two:
                r[2]()

        def t6():
            for r in two:
                r[3]()
            for r in one + two:
                r[4]()

        return t1, t2, t3, t4, t5, t6

    def reduce_ring(buf, a, r2, r1, cs, bs, rows, base):
        g, p, k = Group(6, base), a.pos, a.k
        first = ALL if k == 4 else 0
        across, beside = up(p, 2), (up(p, 1), up(p, 3))

        def half(q, h):
            at = a.half(q, h)
            return buf.at[at + (ALL,) * (5 - len(at)) + (cs,)]

        def elem(q, n, h):
            return a.elem(q, n, h) + (ALL, cs)

        def far(i):
            return r2.at[i, first, rows, bs]

        def near(i, h):
            return r1.at[i, first, h, rows, bs]

        def loop(fn):
            if k == 1:
                fn(0)
            else:
                pl.loop(0, k)(fn)

        def s1():
            for i in (0, 1):
                g.run(lambda i=i: (half(across, i), far(i)), a.dev[i], i)

        def direct(i):
            g.run(lambda: (half(beside[i], 1 - i), near(i, 1 - i)), a.dev[i], 2 + i)

        def s2(i):
            g.got(far(i), i)
            to = beside[i]

            def add(n):
                at = elem(to, n, i)
                buf[at] = buf[at] + r2[i, n, rows, bs]

            loop(add)
            g.run(lambda: (half(to, i), near(i, i)), a.dev[i], 4 + i)

        def s3():
            for i in (0, 1):
                g.got(near(i, 1 - i), 2 + i)
                g.got(near(i, i), 4 + i)

            def add(n):
                for h in (0, 1):
                    at = elem(p, n, h)
                    total = (
                        buf[at].astype(F32)
                        + r1[0, n, h, rows, bs].astype(F32)
                        + r1[1, n, h, rows, bs].astype(F32)
                    )
                    buf[at] = total.astype(BF)

            loop(add)

        return s1, direct, s2, s3, g.end

    def scatter(buf, bufs, base, cs, bs=None, rows=ALL):
        bs = cs if bs is None else bs
        one = [
            reduce_ring(buf, a_y, bufs[0].at[0], bufs[1].at[0], cs, bs, rows, base),
            reduce_ring(buf, b_x, bufs[0].at[1], bufs[1].at[1], cs, bs, rows, base + 6),
        ]
        two = [
            reduce_ring(buf, a_x, bufs[2].at[0], bufs[3].at[0], cs, bs, rows, base + 12),
            reduce_ring(buf, b_y, bufs[2].at[1], bufs[3].at[1], cs, bs, rows, base + 18),
        ]

        def t0():
            for r in one:
                r[0]()

        def t1(i):
            for r in one:
                r[1](i)

        def t2(i):
            for r in one:
                r[2](i)

        def t3():
            for r, q in zip(one, two):
                r[3]()
                q[0]()
                q[1](0)
                q[1](1)

        def t4():
            for i in (0, 1):
                for r in two:
                    r[2](i)

        def t5():
            for r in two:
                r[3]()
            for r in one + two:
                r[4]()

        def start():
            t0()
            t1(0)
            t1(1)

        def onward():
            t2(0)
            t2(1)

        return SimpleNamespace(t0=t0, t1=t1, t2=t2, t3=t3, t4=t4, t5=t5, start=start, onward=onward)

    def place(zz, cc):
        return (lax.rem(zz, 2) * 2 + cc, lax.div(zz, 2))

    half_rows = (slice(0, 32), slice(32, 64))

    rows_base = ids(8)

    def reduce_rows(pb, rsib, rz):
        g = Group(8, rows_base)

        def mine(zz, h):
            return pb.at[place(zz, c) + (half_rows[h],)]

        def s0():
            for i, t in enumerate((zl, 1 - zl)):
                g.go(pb.at[t * 2 + 1 - c], rsib.at[t], sib, i)

        def s1():
            def add(zz):
                at = place(zz, c)
                pb[at] = pb[at] + rsib[lax.rem(zz, 2), lax.div(zz, 2)]

            g.got(rsib.at[zl], 0)
            add(zs[2])
            for i in (0, 1):
                g.go(mine(zs[2], i), rz.at[2, half_rows[i]], zdev[i], 2 + i)
            g.got(rsib.at[1 - zl], 1)
            for i in (0, 1):
                add(zs[i])
                g.go(mine(zs[i], 1 - i), rz.at[i, half_rows[1 - i]], zdev[i], 4 + i)
            add(z)

        def s2():
            for i in (0, 1):
                rows = half_rows[i]
                g.got(rz.at[2, rows], 2 + i)
                at = place(zs[i], c) + (rows,)
                pb[at] = pb[at] + rz[2, rows]
                g.go(mine(zs[i], i), rz.at[i, rows], zdev[i], 6 + i)

        def s3():
            for i in (0, 1):
                g.got(rz.at[i, half_rows[1 - i]], 4 + i)
                g.got(rz.at[i, half_rows[i]], 6 + i)

        def total(rows):
            v = pb[me, zh, rows].astype(F32)
            return v + rz[0, rows].astype(F32) + rz[1, rows].astype(F32)

        return SimpleNamespace(s0=s0, s1=s1, s2=s2, s3=s3, end=g.end, total=total)

    spread_base = ids(10)

    def gather_rows(buf):
        g = Group(10, spread_base)

        def at(zz, h):
            return buf.at[place(zz, c) + (half_rows[h],)]

        def s0():
            for i, (h, d) in enumerate(((0, 0), (1, 1), (1, 0), (0, 1))):
                g.go(at(z, h), at(z, h), zdev[d], i)
            own = buf.at[place(z, c)]
            g.go(own, own, sib, 6)

        def s1():
            g.got(at(zs[1], 0), 0)
            g.go(at(zs[1], 0), at(zs[1], 0), zdev[0], 4)
            g.got(at(zs[0], 1), 1)
            g.go(at(zs[0], 1), at(zs[0], 1), zdev[1], 5)

        def s2():
            def hand_on(zz, i):
                whole = buf.at[place(zz, c)]
                g.go(whole, whole, sib, i)

            g.got(at(zs[1], 1), 2)
            hand_on(zs[1], 7)
            g.got(at(zs[0], 0), 3)
            hand_on(zs[0], 8)
            g.got(at(zs[2], 0), 4)
            g.got(at(zs[2], 1), 5)
            hand_on(zs[2], 9)

        def s3():
            for i, zz in ((6, z), (7, zs[1]), (8, zs[0]), (9, zs[2])):
                g.got(buf.at[place(zz, 1 - c)], i)

        return SimpleNamespace(s0=s0, s1=s1, s2=s2, s3=s3, end=g.end)

    def gather_blocks(buf):
        g = Group(5)

        def s0():
            g.go(buf.at[me, 0], buf.at[me, 0], part, 0)
            g.go(buf.at[me, 1], buf.at[me, 1], other, 1)
            g.go(buf.at[me], buf.at[me], sib, 2)

        def s1():
            for h in (0, 1):
                at = buf.at[(1 - zl) * 2 + c, h]
                g.got(at, h)
                g.go(at, at, sib, 3 + h)

        def s2():
            g.got(buf.at[zl * 2 + 1 - c], 2)
            for h in (0, 1):
                g.got(buf.at[(1 - zl) * 2 + 1 - c, h], 3 + h)

        return s0, s1, s2, g.end

    def twin(buf):
        g = Group(1)

        def start():
            g.go(buf.at[zh], buf.at[zh], zdev[2], 0)

        def wait():
            g.got(buf.at[1 - zh], 0)
            g.end()

        return start, wait

    for i in range(4):
        R.wla[i, :, 0:256] = R.qw[:, i * 256 : (i + 1) * 256]
        R.wla[i, :, 256:384] = R.kw[:, i * 128 : (i + 1) * 128]
        R.wla[i, :, 384:512] = R.vw[:, i * 128 : (i + 1) * 128]
    pairs, rings = [ids(3) for _ in range(4)], [ids(24) for _ in range(5)]
    ex_a = exchange(R.wa, R.wla, pairs[0])
    ex_o = exchange(R.wo, R.wlo, pairs[1])
    ex_m = exchange(R.wm, R.wlm, pairs[2], slice(0, 1536))
    ex_d = exchange(R.wm, R.wlm, pairs[3], slice(1536, 2304))
    ag_a, ag_o = gather(R.wa, rings[0]), gather(R.wo, rings[1])
    ag_m = gather(R.wm, rings[2], slice(0, 1536))
    ag_d = gather(R.wm, rings[3], slice(1536, 2304))
    ag_x = gather_blocks(R.xn)
    ag_c = gather_blocks(R.cot)
    ag_kv = gather(R.kv, rings[4])

    pl.semaphore_wait(barrier, len(greet))
    ex_a[0]()
    for i in range(4):
        R.wlo[i, :, 0:256] = R.ow[:, i * 256 : (i + 1) * 256]
        pick = select(lambda r, q, i=i: (r == q + 2 * i) & (q < 2), (8, 128))
        R.wlo[i, :, 256:384] = mm(R.gw[...].T, pick).astype(BF)
        R.wlm[i, :, 1536:2304] = R.fd[:, i * 768 : (i + 1) * 768]
    ex_o[0]()
    ex_d[0]()

    @pl.loop(0, 4)
    def _(t):
        rows = pl.ds(pl.multiple_of(lax.rem(t, 2) * 32, 32), 32)
        v = R.x[pl.ds(pl.multiple_of(t * 32, 32), 32), :].astype(F32)
        R.xn[me, lax.div(t, 2), rows] = (v * rms_scale(v) * R.ag[...]).astype(BF)

    ag_x[0]()
    for i in range(4):
        R.wlm[i, :, 0:768] = R.fg[:, i * 768 : (i + 1) * 768]
        R.wlm[i, :, 768:1536] = R.fu[:, i * 768 : (i + 1) * 768]
    ex_m[0]()
    first = lax.broadcasted_iota(jnp.int32, (128, 128), 1) < 64
    for i in range(4):
        base = (i // 2) * 32 + j * 2 + i % 2
        cb, sb = R.cb[pl.ds(base, 1), :], R.sb[pl.ds(base, 1), :]
        sin = sb * R.cr[...] + cb * R.sr[...]
        R.cos[i] = cb * R.cr[...] - sb * R.sr[...]
        R.sin[i] = jnp.where(first, -sin, sin)
    R.cot[me] = R.ct[...].reshape(2, 64, WIDTH)
    ex_a[1]()
    ag_a[0]()
    ex_o[1]()
    ag_o[0]()
    ag_a[1]()
    ex_d[1]()
    ag_d[0]()
    ag_o[1]()
    ag_x[1]()
    ag_a[2]()
    ag_d[1]()
    ag_x[2]()
    ag_a[3]()
    ex_m[1]()
    ag_m[0]()
    ag_a[4]()
    ag_a[5]()

    @pl.loop(0, 2)
    def _(zi):
        w = R.wa[...].reshape(WIDTH, PROJ)
        both = mm(R.xn[pl.ds(zi * 2, 2)].reshape(256, WIDTH), w)
        for ci in (0, 1):
            i, raw = zi * 2 + ci, both[ci * 128 : (ci + 1) * 128]
            cos, sin = R.cos[i], R.sin[i]
            R.qraw[i] = raw[:, 0:256]
            R.kraw[i] = raw[:, 256:384]
            for h in (0, 1):
                v = raw[:, h * 128 : (h + 1) * 128]
                q = rope(v * rms_scale(v) * R.qg[...], cos, sin) * (SCALE * LOG2E)
                R.qx[zi, h, ci, :, 0:128] = q.astype(BF)
            v = raw[:, 256:384]
            k = rope(v * rms_scale(v) * R.kg[...], cos, sin)
            R.kv[zi, y, x, ci, :, 0:128] = k.astype(BF)
            R.kv[zi, y, x, ci, :, 128:256] = raw[:, 384:512].astype(BF)

    ag_kv[0]()
    ag_c[0]()
    ag_m[1]()

    ones = jnp.ones((256, 128), BF)
    key_i = lax.broadcasted_iota(jnp.int32, (512, 256), 1)
    row_i = lax.broadcasted_iota(jnp.int32, (512, 256), 0)
    seen = key_i <= lax.rem(row_i, 256)
    R.oacc[...] = jnp.zeros((2, 512, 256), F32)

    def keys_of(at):
        return R.kv[at + (ALL, ALL, slice(0, 128))].reshape(256, 128)

    def values_of(at):
        v = R.kv[at + (ALL, ALL, slice(128, 256))].reshape(256, 128)
        return jnp.concatenate([v, ones], axis=1)

    def forward(tiles):
        work = []
        for g in (0, 1):
            mine = [u for u in tiles if g in u[1]]
            if mine:
                k = jnp.concatenate([keys_of(u[0]) for u in mine], axis=0)
                v = jnp.concatenate([values_of(u[0]) for u in mine], axis=0)
                scores = mm_tb(R.qx[g, :, :, :, 0:128].reshape(512, 128), k)
                work.append((g, mine, v, scores))
        for g, mine, v, scores in work:
            p = jnp.exp2(scores)
            if any(u[2] == g for u in mine):
                parts = [p[:, i * 256 : (i + 1) * 256] for i in range(len(mine))]
                parts = [jnp.where(seen, q, 0.0) if u[2] == g else q for u, q in zip(mine, parts)]
                p = jnp.concatenate(parts, axis=1)
            R.oacc[g] += mm(p.astype(BF), v)

    def tile_pair(fn, empty, at0, at1):
        t0, t1 = at0[0] * 4 + at0[1], at1[0] * 4 + at1[1]
        at0, at1 = (0,) + at0, (1,) + at1

        @pl.when((t0 < j) & (t1 < j))
        def _():
            fn([(at0, (0, 1), None), (at1, (1,), None)])

        @pl.when((t0 < j) & (t1 > j))
        def _():
            fn([(at0, (0, 1), None)])

        @pl.when((t0 > j) & (t1 < j))
        def _():
            fn([(at0, (1,), None), (at1, (1,), None)])

        @pl.when((t0 > j) & (t1 > j))
        def _():
            fn([(at0, (1,), None)])

        if empty is not None:

            @pl.when(t1 > j)
            def _():
                empty(at1)

    own = [((0, y, x), (0, 1), 0), ((1, y, x), (1,), 1)]

    def near(fn, empty=None):
        @pl.loop(1, 4)
        def _(k):
            tile_pair(fn, empty, (y, up(x, k)), (up(y, k), x))

    def side(fn, a, empty=None):
        @pl.loop(0, 4)
        def _(k):
            tile_pair(fn, empty, (up(y, a), k), (k, up(x, a)))

    forward(own)
    ag_kv[1]()
    ag_kv[2]()
    near(forward)
    ag_c[1]()
    ag_kv[3]()
    ag_o[2]()
    ag_kv[4]()

    @pl.loop(0, 3)
    def _(k):
        @pl.when(k == 2)
        def _():
            ag_o[3]()
            ag_m[2]()
            ag_kv[5]()

        side(forward, 1 + 2 * k - 3 * lax.div(k, 2))

    ag_o[4]()
    ag_o[5]()

    @pl.loop(0, 2)
    def _(zi):
        w = R.wo[:, :, :, :, :, 256:384].reshape(WIDTH, 128)
        v = mm(R.xn[pl.ds(zi * 2, 2)].reshape(256, WIDTH), w)
        R.gl[pl.ds(zi * 2, 2)] = v.reshape(2, 128, 128)

    lanes = lax.broadcasted_iota(jnp.int32, (128, 128), 1)

    @pl.loop(0, 4)
    def _(i):
        zi, ci = lax.div(i, 2), lax.rem(i, 2)
        for h in (0, 1):
            rows = pl.ds(pl.multiple_of(h * 256 + ci * 128, 128), 128)
            total = R.oacc[zi, rows, 128:256]
            a = R.oacc[zi, rows, 0:128] / total
            R.att[i, :, h * 128 : (h + 1) * 128] = a
            R.qx[zi, h, ci, :, 128:256] = three_parts(-jnp.log2(total), lanes)
            gate = jax.nn.sigmoid(R.gl[i][:, h : h + 1])
            R.gated[i, :, h * 128 : (h + 1) * 128] = (a * gate).astype(BF)

    def spread(n, value):
        cols = pl.ds(pl.multiple_of(n * 256, 256), 256)
        return cols, value.reshape(4, 2, 64, 256).astype(BF)

    rs1 = reduce_rows(R.pb, R.rsib, R.rz)
    ag_n = gather_rows(R.nm)

    def project(cc):
        rows = jnp.concatenate([R.gated[cc], R.gated[2 + cc]], axis=0)

        @pl.loop(0, 8, unroll=4)
        def _(n):
            w = R.wo[lax.div(n, 4), lax.rem(n, 4), :, :, :, 0:256].reshape(256, 256)
            cols = pl.ds(pl.multiple_of(n * 256, 256), 256)
            v = mm_tb(rows, w).astype(BF).reshape(2, 2, 64, 256)
            R.pb[cc, :, :, cols] = v[0]
            R.pb[2 + cc, :, :, cols] = v[1]

    project(1 - c)
    rs1.s0()
    project(c)
    rs1.s1()
    rs1.s2()
    ag_m[3]()
    ag_d[2]()
    rs1.s3()

    def owned(t):
        return pl.ds(pl.multiple_of(t * 16, 16), 16)

    @pl.loop(0, 4)
    def _(t):
        rows = owned(t)
        v = R.x[pl.ds(pl.multiple_of(zh * 64 + t * 16, 16), 16), :].astype(F32)
        v = v + rs1.total(rows)
        R.hid[rows] = v
        R.nm[me, zh, rows] = (v * rms_scale(v) * R.fgain[...]).astype(BF)

    rs1.end()
    for g in (ex_a, ex_o, ex_m, ex_d):
        g[2]()
    ag_n.s0()
    ag_c[2]()
    ag_n.s1()
    ag_m[4]()
    ag_n.s2()
    ag_m[5]()
    ag_d[3]()
    ag_n.s3()

    def weight(k, n):
        at = pl.ds(pl.multiple_of(k * 768 + n * 256, 256), 256)
        return R.wm[:, :, :, :, :, at].reshape(WIDTH, 256)

    @pl.loop(0, 3, unroll=3)
    def _(n):
        cols = pl.ds(pl.multiple_of(n * 256, 256), 256)
        rows = R.nm[...].reshape(512, WIDTH)
        gate = mm(rows, weight(0, n))
        upper = mm(rows, weight(1, n))
        sg = jax.nn.sigmoid(gate)
        silu = gate * sg
        R.act[0, :, cols] = (upper * (sg * (1.0 + gate * (1.0 - sg)))).astype(BF)
        R.act[1, :, cols] = silu.astype(BF)
        R.act[2, :, cols] = (silu * upper).astype(BF)

    def block(n):
        return (lax.div(n, 4), lax.rem(n, 4), ALL, ALL, ALL)

    def turned(ref, n):
        cols = pl.ds(pl.multiple_of(n * 256, 256), 256)
        return ref[:, :, :, cols].reshape(512, 256).T

    big = (R.m_r2, R.m_r1, R.m_q2, R.m_q1)
    rs_d = scatter(R.ga, big, rings[0], slice(0, 768))
    rs_m = scatter(R.wm, big, rings[1], slice(0, 1536), slice(768, 2304))

    @pl.loop(0, 8, unroll=4)
    def _(n):
        g = mm(turned(R.cot, n), R.act[2])
        R.ga[block(n) + (slice(0, 768),)] = g.astype(BF).reshape(4, 2, 32, 768)

    rs_d.start()
    ag_d[4]()
    ag_d[5]()

    @pl.loop(0, 3, unroll=3)
    def _(n):
        cols = pl.ds(pl.multiple_of(n * 256, 256), 256)
        grad = mm(R.cot[...].reshape(512, WIDTH), weight(2, n))
        R.act[0, :, cols] = (grad * R.act[0, :, cols].astype(F32)).astype(BF)
        R.act[1, :, cols] = (grad * R.act[1, :, cols].astype(F32)).astype(BF)

    @pl.loop(0, 8, unroll=4)
    def _(n):
        at = block(n)
        v = mm_tb(R.act[0], R.wm[at + (slice(0, 768),)].reshape(256, 768))
        v = v + mm_tb(R.act[1], R.wm[at + (slice(768, 1536),)].reshape(256, 768))
        cols, v = spread(n, v)
        R.pb[:, :, :, cols] = v

    rs2 = reduce_rows(R.pb, R.rsib, R.rz)
    rs_f = reduce_rows(R.pb2, R.rsib, R.rz)
    rs2.s0()

    def feed_weights(n):
        at = block(n)
        t = turned(R.nm, n)
        R.wm[at + (slice(0, 768),)] = mm(t, R.act[0]).astype(BF).reshape(4, 2, 32, 768)
        R.wm[at + (slice(768, 1536),)] = mm(t, R.act[1]).astype(BF).reshape(4, 2, 32, 768)

    pl.loop(0, 4, unroll=4)(feed_weights)
    rs2.s1()
    rs_d.onward()
    pl.loop(4, 8, unroll=4)(feed_weights)
    rs2.s2()

    def tell(devices, sem):
        for d in devices:
            pl.semaphore_signal(sem, inc=1, device_id=d, device_id_type=MESH)

    group = [sib] + zdev
    ring = xdev[:2] + ydev[:2]
    ag_n.end()
    tell(group, R.free.at[0])
    ag_h = gather_rows(R.nm)
    rs_m.start()

    @pl.loop(0, 8, unroll=4)
    def _(n):
        w = R.wm[block(n) + (slice(1536, 2304),)].reshape(256, 768)
        cols, v = spread(n, mm_tb(R.act[2], w))
        R.pb2[:, :, :, cols] = v

    R.dgs[...] = jnp.zeros((2, WIDTH), F32)
    ag_c[3]()
    rs2.s3()
    pl.semaphore_wait(R.free.at[0], 4)

    @pl.loop(0, 4)
    def _(t):
        rows = owned(t)
        dv, dg = rms_back(R.hid[rows], R.fgain[...], rs2.total(rows))
        dh = dv + R.ct[pl.ds(pl.multiple_of(zh * 64 + t * 16, 16), 16), :].astype(F32)
        R.dgs[1:2, :] += dg
        R.gh[rows] = dh
        R.nm[me, zh, rows] = dh.astype(BF)

    rs2.end()
    ag_h.s0()
    rs_d.t3()
    ag_h.s1()
    rs_m.onward()
    ag_h.s2()
    ag_h.s3()
    rs_f.s0()

    @pl.loop(0, 2)
    def _(zi):
        w = R.wo[:, :, :, :, :, 0:256].reshape(WIDTH, 256)
        both = mm(R.nm[pl.ds(zi * 2, 2)].reshape(256, WIDTH), w)
        for ci in (0, 1):
            i, grad = zi * 2 + ci, both[ci * 128 : (ci + 1) * 128]
            logits = jnp.zeros((128, 128), F32)
            for h in (0, 1):
                gate = jax.nn.sigmoid(R.gl[i][:, h : h + 1])
                gr = grad[:, h * 128 : (h + 1) * 128]
                a = R.att[i, :, h * 128 : (h + 1) * 128]
                low = (gr * gate).astype(BF)
                dl = jnp.sum(gr * a, axis=1, keepdims=True) * (gate * (1.0 - gate))
                logits = jnp.where(lanes == h, dl, logits)
                delta = jnp.sum(low.astype(F32) * a, axis=1, keepdims=True)
                R.dox[zi, h, ci, :, 0:128] = low
                R.dox[zi, h, ci, :, 128:256] = three_parts(-delta, lanes)
            R.gsc[i, :, 512:640] = logits.astype(BF)

    rs_d.t4()
    rs_f.s1()

    R.oacc[...] = jnp.zeros((2, 512, 256), F32)
    row_t = lax.broadcasted_iota(jnp.int32, (256, 512), 1)
    key_t = lax.broadcasted_iota(jnp.int32, (256, 512), 0)
    seen_t = key_t <= lax.rem(row_t, 256)

    def backward(tiles):
        at = [u[0] for u in tiles]
        k = [keys_of(u) for u in at]
        kx = [jnp.concatenate([u, ones], axis=1) for u in k]
        vx = [values_of(u) for u in at]
        kt = [u.T for u in k]
        q = [R.qx[g].reshape(512, 256) for g in (0, 1)]
        d = [R.dox[g].reshape(512, 256) for g in (0, 1)]
        units = [(i, g, u[2] == g) for i, u in enumerate(tiles) for g in u[1]]
        p = [mm_tb(kx[i], q[g]) for i, g, _ in units]
        dp = [mm_tb(vx[i], d[g]) for i, g, _ in units]
        p = [jnp.exp2(u) for u in p]
        p = [jnp.where(seen_t, u, 0.0) if cut else u for u, (_, _, cut) in zip(p, units)]
        ds = [(u * w).astype(BF) for u, w in zip(p, dp)]
        p = [u.astype(BF) for u in p]
        dv = [mm(u, d[g][:, 0:128]) for u, (_, g, _) in zip(p, units)]
        dk = [mm(u, q[g][:, 0:128]) for u, (_, g, _) in zip(ds, units)]
        dq = [mm(kt[i], u) for u, (i, _, _) in zip(ds, units)]
        for g in (0, 1):
            mine = [u for u, (_, h, _) in zip(dq, units) if h == g]
            if mine:
                total = sum(mine[1:], mine[0])
                R.oacc[g, 0:128] += total[:, 0:256]
                R.oacc[g, 128:256] += total[:, 256:512]
        for i, place in enumerate(at):
            mine = [n for n, u in enumerate(units) if u[0] == i]
            first, rest = mine[0], mine[1:]
            total = sum([dk[n] for n in rest], dk[first])
            R.kv[place + (ALL, ALL, slice(0, 128))] = total.astype(BF).reshape(2, 128, 128)
            total = sum([dv[n] for n in rest], dv[first])
            R.kv[place + (ALL, ALL, slice(128, 256))] = total.astype(BF).reshape(2, 128, 128)

    def nothing(at):
        R.kv[at] = jnp.zeros((2, 128, 256), BF)

    small = (R.k_r2, R.k_r1, R.k_q2, R.k_q1)
    rs_k = scatter(R.kv, small, rings[4], slice(0, 256))

    @pl.loop(0, 3)
    def _(k):
        side(backward, 2 - k + 3 * lax.div(k, 2), nothing)

        @pl.when(k == 0)
        def _():
            rs_k.t0()

        @pl.when(k == 1)
        def _():
            rs_k.t1(0)

        @pl.when(k == 2)
        def _():
            rs_k.t1(1)

    rs_f.s2()
    rs_k.t2(0)
    rs_k.t2(1)
    rs_m.t3()
    rs_d.t5()
    tell(ring, R.free.at[2])
    R.wm[:, y, x, :, :, 1536:2304] = R.ga[:, y, x, :, :, 0:768]
    near(backward, nothing)
    backward(own)
    rs_f.s3()
    tw_o = twin(R.ob)

    @pl.loop(0, 4)
    def _(t):
        rows = owned(t)
        R.ob[zh, rows] = (R.hid[rows] + rs_f.total(rows)).astype(BF)

    rs_f.end()
    tell(group, R.free.at[1])
    tw_o[0]()

    rs_k.t3()

    R.dgh[...] = jnp.zeros((8, 128), F32)

    @pl.loop(0, 4)
    def _(i):
        zi, ci = lax.div(i, 2), lax.rem(i, 2)
        for h in (0, 1):
            cols = pl.ds(pl.multiple_of(ci * 128, 128), 128)
            dq = R.oacc[zi, h * 128 : (h + 1) * 128, cols].T * SCALE
            dq = rope_back(dq, R.cos[i], R.sin[i])
            dv, dg = rms_back(R.qraw[i, :, h * 128 : (h + 1) * 128], R.qg[...], dq)
            R.dgh[0:1, :] += dg
            R.gsc[i, :, h * 128 : (h + 1) * 128] = dv.astype(BF)

    rs_m.t4()

    @pl.loop(0, 8, unroll=4)
    def _(n):
        at = block(n)
        g = mm(turned(R.nm, n), R.gated[...].reshape(512, 256))
        R.ga[at + (slice(0, 256),)] = g.astype(BF).reshape(4, 2, 32, 256)
        t = turned(R.xn, n)
        g = mm(t, R.gsc[:, :, 0:256].reshape(512, 256))
        R.ga[at + (slice(256, 512),)] = g.astype(BF).reshape(4, 2, 32, 256)
        g = mm(t, R.gsc[:, :, 512:640].reshape(512, 128))
        R.ga[at + (slice(512, 640),)] = g.astype(BF).reshape(4, 2, 32, 128)

    rs_e = scatter(R.ga, big, rings[2], slice(0, 640))
    pl.semaphore_wait(R.free.at[2], 4)
    rs_k.t4()
    rs_e.start()
    rs_k.t5()

    @pl.loop(0, 4)
    def _(i):
        zi, ci = lax.div(i, 2), lax.rem(i, 2)
        dk = R.kv[zi, y, x, ci, :, 0:128].astype(F32) * LN2
        dk = rope_back(dk, R.cos[i], R.sin[i])
        dv, dg = rms_back(R.kraw[i], R.kg[...], dk)
        R.dgh[1:2, :] += dg
        R.gsc[i, :, 256:384] = dv.astype(BF)
        R.gsc[i, :, 384:512] = R.kv[zi, y, x, ci, :, 128:256]

    @pl.loop(0, 8, unroll=4)
    def _(n):
        g = mm(turned(R.xn, n), R.gsc[:, :, 256:512].reshape(512, 256))
        R.ga[block(n) + (slice(640, 896),)] = g.astype(BF).reshape(4, 2, 32, 256)

    rs_l = scatter(R.ga, small, rings[3], slice(640, 896), slice(0, 256), slice(0, 32))
    rs_l.start()
    rs_m.t5()
    gb_m = give_back(R.wm, R.wlm, pairs[0])
    gb_m[0]()

    @pl.loop(0, 8, unroll=4)
    def _(n):
        at = block(n)
        v = mm_tb(R.gsc[:, :, 0:512].reshape(512, 512), R.wa[at].reshape(256, PROJ))
        w = R.wo[at + (slice(256, 384),)].reshape(256, 128)
        v = v + mm_tb(R.gsc[:, :, 512:640].reshape(512, 128), w)
        cols = pl.ds(pl.multiple_of(n * 256, 256), 256)
        dg = jnp.sum(v * R.xn[:, :, :, cols].reshape(512, 256).astype(F32), axis=0, keepdims=True)
        R.dgs[0:1, cols] = dg / R.ag[:, cols]
        cols, v = spread(n, v)
        R.pb[:, :, :, cols] = v

    rs3 = reduce_rows(R.pb, R.rsib, R.rz)
    pl.semaphore_wait(R.free.at[1], 4)
    rs3.s0()

    for r in range(16):
        R.sums[0, r : r + 1, :] = R.dgs[0:1, r * 128 : (r + 1) * 128]
        R.sums[0, 16 + r : 17 + r, :] = R.dgs[1:2, r * 128 : (r + 1) * 128]
    R.sums[0, 32:40, :] = R.dgh[...]

    def add_up(stage, devices):
        g, first = Group(len(devices)), (0, 7, 10)[stage]
        for i, d in enumerate(devices):
            g.go(R.sums.at[stage], R.came.at[first + i], d, i)

        def finish():
            v = R.sums[stage]
            for i in range(len(devices)):
                g.got(R.came.at[first + i], i)
                v = v + R.came[first + i]
            R.sums[stage + 1] = v
            g.end()

        return finish

    fin = add_up(0, group + zsib)
    rs_e.onward()
    rs3.s1()
    rs_l.onward()
    rs3.s2()
    fin()
    fin = add_up(1, xdev)
    rs_e.t3()
    fin()
    fin = add_up(2, ydev)
    rs_l.t3()
    rs3.s3()
    tw_i = twin(R.ib)

    @pl.loop(0, 4)
    def _(t):
        rows = owned(t)
        v = R.x[pl.ds(pl.multiple_of(zh * 64 + t * 16, 16), 16), :].astype(F32)
        dv, _ = rms_back(v, R.ag[...], rs3.total(rows))
        R.ib[zh, rows] = (R.gh[rows] + dv).astype(BF)

    tw_i[0]()
    rs3.end()
    rs_e.t4()
    rs_l.t4()
    def put(i, src, dst):
        cp = pltpu.make_async_copy(src, dst, R.put.at[i])
        cp.start()
        return cp

    gb_m[1]()
    puts = [put(0, R.wlm, R.o_fm)]
    tw_o[1]()
    puts.append(put(1, R.ob, R.o_out))
    fin()
    puts.append(put(2, R.sums.at[3], R.o_gain))
    rs_e.t5()
    rs_l.t5()
    gb_a = give_back(R.ga, R.wl8, pairs[1])
    gb_a[0]()
    tw_i[1]()
    puts.append(put(3, R.ib, R.o_in))
    gb_a[1]()
    puts.append(put(4, R.wl8, R.o_fa))
    for cp in puts:
        cp.wait()
    ag_x[3]()
    ag_h.end()
    gb_m[2]()
    gb_a[2]()
    assert count[0] == COPIES, count


INPUTS = [
    *("x", "ct", "ag", "qg", "kg", "fgain"),
    *("qw", "kw", "vw", "gw", "ow", "fg", "fu", "fd"),
    *("cr", "sr", "cb", "sb"),
]
OUTPUTS = [
    ("o_out", (2, 64, WIDTH), BF),
    ("o_in", (2, 64, WIDTH), BF),
    ("o_gain", (40, 128), F32),
    ("o_fm", (4, 32, 2304), BF),
    ("o_fa", (4, 32, ATT), BF),
]
RESULTS = [
    ((128, WIDTH), BF),
    ((128, WIDTH), BF),
    ((1, 32), F32),
    ((32, 1024), F32),
    ((32, 512), F32),
    ((32, 512), F32),
    ((8, 32), F32),
    ((1, 128), F32),
    ((1, 128), F32),
    ((32, 1024), F32),
    ((1, 32), F32),
    ((32, 3072), F32),
    ((32, 3072), F32),
    ((32, 3072), F32),
]
SCRATCH = [
    ("wla", (4, 32, PROJ), BF),
    ("wlo", (4, 32, 384), BF),
    ("wl8", (4, 32, ATT), BF),
    ("wlm", (4, 32, 2304), BF),
    ("wa", (2, 4, 4, 2, 32, PROJ), BF),
    ("wo", (2, 4, 4, 2, 32, 384), BF),
    ("ga", (2, 4, 4, 2, 32, ATT), BF),
    ("wm", (2, 4, 4, 2, 32, 2304), BF),
    ("kv", (2, 4, 4, 2, 128, 256), BF),
    ("xn", (4, 2, 64, WIDTH), BF),
    ("cot", (4, 2, 64, WIDTH), BF),
    ("nm", (4, 2, 64, WIDTH), BF),
    ("cos", (4, 128, 128), F32),
    ("sin", (4, 128, 128), F32),
    ("qraw", (4, 128, 256), F32),
    ("kraw", (4, 128, 128), F32),
    ("gl", (4, 128, 128), F32),
    ("qx", (2, 2, 2, 128, 256), BF),
    ("dox", (2, 2, 2, 128, 256), BF),
    ("oacc", (2, 512, 256), F32),
    ("att", (4, 128, 256), F32),
    ("gated", (4, 128, 256), BF),
    ("gsc", (4, 128, 640), BF),
    ("act", (3, 512, 768), BF),
    ("hid", (64, WIDTH), F32),
    ("gh", (64, WIDTH), F32),
    ("dgs", (2, WIDTH), F32),
    ("dgh", (8, 128), F32),
    ("pb", (4, 2, 64, WIDTH), BF),
    ("pb2", (4, 2, 64, WIDTH), BF),
    ("rsib", (2, 2, 64, WIDTH), BF),
    ("rz", (3, 64, WIDTH), BF),
    ("m_r2", (2, 2, 4, 32, 2304), BF),
    ("m_r1", (2, 2, 4, 2, 32, 2304), BF),
    ("m_q2", (2, 2, 1, 32, 2304), BF),
    ("m_q1", (2, 2, 1, 2, 32, 2304), BF),
    ("k_r2", (2, 2, 4, 128, 256), BF),
    ("k_r1", (2, 2, 4, 2, 128, 256), BF),
    ("k_q2", (2, 2, 1, 128, 256), BF),
    ("k_q1", (2, 2, 1, 2, 128, 256), BF),
    ("ob", (2, 64, WIDTH), BF),
    ("ib", (2, 64, WIDTH), BF),
    ("sums", (4, 40, 128), F32),
    ("came", (13, 40, 128), F32),
]
COPIES = 175


def kernel(*refs):
    names = INPUTS + [o[0] for o in OUTPUTS] + [v[0] for v in SCRATCH] + ["send", "recv", "free", "put"]
    body(SimpleNamespace(**dict(zip(names, refs))))


def finish(out, grad_in, gain, fm, fa, *to):
    to[0][...] = out[...].reshape(128, WIDTH)
    to[1][...] = grad_in[...].reshape(128, WIDTH)
    place = lax.axis_index("seq")
    for at, first in ((2, 0), (10, 16)):
        v = gain[pl.ds(first + lax.div(place, 4), 1), :]
        to[at][...] = pltpu.roll(v, lax.rem(128 - lax.rem(place, 4) * 32, 128), 1)[:, 0:32]
    to[7][...] = gain[32:33, :]
    to[8][...] = gain[33:34, :]
    gates = jnp.zeros((8, 32), F32)
    for i in range(4):
        wide = slice(i * 256, (i + 1) * 256)
        low = slice(i * 128, (i + 1) * 128)
        to[9][:, wide] = fa[i, :, 0:256].astype(F32)
        to[3][:, wide] = fa[i, :, 256:512].astype(F32)
        to[4][:, low] = fa[i, :, 640:768].astype(F32)
        to[5][:, low] = fa[i, :, 768:896].astype(F32)
        pick = select(lambda r, q, i=i: (r == q + 2 * i) & (q < 2), (8, 128))
        gates = gates + mm_tb(pick, fa[i, :, 512:640])
        for k in range(3):
            cols = slice(k * 768, (k + 1) * 768)
            to[11 + k][:, i * 768 : (i + 1) * 768] = fm[i, :, cols].astype(F32)
    to[6][...] = gates


def rope_tables():
    inverse = ROPE_BASE ** (-np.arange(HEAD // 2) * 2.0 / HEAD)
    inverse = np.concatenate([inverse, inverse]).astype(np.float32).astype(np.float64)
    rows = np.arange(128)[:, None] * inverse
    blocks = np.arange(64)[:, None] * 128 * inverse
    return [jnp.asarray(f(a), F32) for a in (rows, blocks) for f in (np.cos, np.sin)]


def per_device(
    inputs,
    attention_gain,
    query_weight,
    key_matrix,
    value_matrix,
    gate_weight,
    query_gain,
    key_gain,
    out_weight,
    feed_gain,
    feed_gate,
    feed_up,
    feed_down,
    cotangent,
):
    vmem = pl.BlockSpec(memory_space=pltpu.VMEM)
    out = pl.pallas_call(
        kernel,
        out_shape=[jax.ShapeDtypeStruct(shape, kind) for _, shape, kind in OUTPUTS],
        in_specs=[vmem] * len(INPUTS),
        out_specs=[pl.BlockSpec(memory_space=pl.ANY)] * len(OUTPUTS),
        scratch_shapes=[pltpu.VMEM(shape, kind) for _, shape, kind in SCRATCH]
        + [pltpu.SemaphoreType.DMA((COPIES,)), pltpu.SemaphoreType.DMA((COPIES,))]
        + [pltpu.SemaphoreType.REGULAR((3,)), pltpu.SemaphoreType.DMA((5,))],
        compiler_params=pltpu.CompilerParams(
            collective_id=0, has_side_effects=True, vmem_limit_bytes=63 * 2**20
        ),
        name="block",
    )(
        inputs,
        cotangent,
        attention_gain.reshape(1, WIDTH),
        query_gain.reshape(1, HEAD),
        key_gain.reshape(1, HEAD),
        feed_gain.reshape(1, WIDTH),
        query_weight,
        key_matrix,
        value_matrix,
        gate_weight.T,
        out_weight.T,
        feed_gate,
        feed_up,
        feed_down.T,
        *rope_tables(),
    )
    out = pl.pallas_call(
        finish,
        out_shape=[jax.ShapeDtypeStruct(shape, kind) for shape, kind in RESULTS],
        compiler_params=pltpu.CompilerParams(vmem_limit_bytes=60 * 2**20),
        name="results",
    )(*out)
    out = list(out)
    for i in (2, 7, 8, 10):
        out[i] = out[i].reshape(-1)
    for i in (6, 9, 13):
        out[i] = out[i].T
    return tuple(out)


def solution(mesh):
    seq, both, turned = P("seq", None), P("seq", "grp"), P("grp", "seq")
    in_specs = (seq, P(), both, both, both, both, P(), P(), turned, P(), both, both, turned, seq)
    out_specs = (
        seq, seq, P("seq"), both, both, both, both, P(), P(), turned, P("seq"), both, both, turned,
    )
    return jax.shard_map(
        per_device, mesh=mesh, in_specs=in_specs, out_specs=out_specs, check_vma=False
    )
```

profile of v0, /device:TPU:1, one launch (start us, length us, event | category | flops | bytes accessed | tf_op | source)
XLA Modules:
  0.0 213.3 jit_solution(11200831581520027520)
XLA Ops:
  0.7 209.6 %block.1 = (bf16[2,64,2048]{2,1,0:T(8,128)(2,1)}, bf16[2,64,2048]{2,1,0:T(8,128)(2,1)}, f32[40,128]{1,0:T(8,128)}, bf16[4,32,2304]{2,1,0:T(8,128)(2,1)}, bf16[4,32,896]{2,1,0:T(8,128)(2,1)}) custom-call(bf16[128,2048]{1,0:T(8,128)(2,1)} %refs_0_.1, bf16[128,2048]{1,0:T(8,128)(2,1)} %refs_1_.1, f32[1,2048]{1,0:T(1,128)} %bitcast.16, f32[1,128]{1,0:T(1,128)} %bitcast.19, ...), custom_call_target="tpu_custom_call" | custom-call | tf_op jit(solution)/shard_map/block/pallas_call | solution.py:1208
  210.3 3.0 %results.1 = (bf16[128,2048]{1,0:T(8,128)(2,1)}, bf16[128,2048]{1,0:T(8,128)(2,1)}, f32[1,32]{1,0:T(1,128)}, f32[32,1024]{1,0:T(8,128)}, f32[32,512]{1,0:T(8,128...) custom-call(bf16[2,64,2048]{2,1,0:T(8,128)(2,1)} %get-tuple-element., ...), custom_call_target="tpu_custom_call" | custom-call | tf_op jit(solution)/shard_map/results/pallas_call | solution.py:1237
where the time goes:
time: 213 us
  Pallas kernels  213 us (100%)
    pallas_call x1, Pallas kernels, per_device(): pl.pallas_call(kernel, out_shape=[jax.ShapeDtypeStruct(shape, kind) for _...  210 us

commit v1 on v0

--- a/solution.py
+++ b/solution.py
@@ -13,7 +13,7 @@
 WIDTH = 2048
 HEAD = 128
 EIGHTH = 768
-ATT = 896
+ATT = 768
 PROJ = 512
 SCALE = HEAD**-0.5
 LOG2E = 1.4426950408889634
@@ -494,11 +494,21 @@
     pl.semaphore_wait(barrier, len(greet))
     ex_a[0]()
     for i in range(4):
-        R.wlo[i, :, 0:256] = R.ow[:, i * 256 : (i + 1) * 256]
-        pick = select(lambda r, q, i=i: (r == q + 2 * i) & (q < 2), (8, 128))
-        R.wlo[i, :, 256:384] = mm(R.gw[...].T, pick).astype(BF)
+        R.wlo[i] = R.ow[:, i * 256 : (i + 1) * 256]
         R.wlm[i, :, 1536:2304] = R.fd[:, i * 768 : (i + 1) * 768]
     ex_o[0]()
+
+    shift = select(lambda r, q: q == r + me * 32, (32, 128))
+    wide = mm(R.gw[...], shift).astype(BF)
+    for i in range(4):
+        pick = select(lambda r, q, i=i: (q == r + 2 * i) & (r < 2), (16, 8))
+        R.gt_l[i] = mm(pick, wide).astype(BF)
+    gates = Group(9)
+    steps = (1, 3, 2)
+    near_group = [(zl * 2 + 1 - c, sib), ((1 - zl) * 2 + c, part), ((1 - zl) * 2 + 1 - c, diag)]
+    R.gt_in[me] = R.gt_l[me]
+    for n, (i, d) in enumerate(near_group):
+        gates.go(R.gt_l.at[i], R.gt_in.at[me], d, n)
     ex_d[0]()
 
     @pl.loop(0, 4)
@@ -524,18 +534,27 @@
     ag_a[0]()
     ex_o[1]()
     ag_o[0]()
+    for n, (i, _) in enumerate(near_group):
+        gates.got(R.gt_in.at[i], n)
+    R.gt[y, x] = (R.gt_in[0] + R.gt_in[1]) + (R.gt_in[2] + R.gt_in[3])
+    for n in range(3):
+        gates.go(R.gt.at[y, x], R.gt.at[y, x], xdev[n], 3 + n)
     ag_a[1]()
     ex_d[1]()
     ag_d[0]()
     ag_o[1]()
+    ag_a[2]()
     ag_x[1]()
-    ag_a[2]()
     ag_d[1]()
-    ag_x[2]()
     ag_a[3]()
+    for n, k in enumerate(steps):
+        gates.got(R.gt.at[y, up(x, 4 - k)], 3 + n)
+    for n in range(3):
+        gates.go(R.gt.at[y], R.gt.at[y], ydev[n], 6 + n)
     ex_m[1]()
     ag_m[0]()
     ag_a[4]()
+    ag_x[2]()
     ag_a[5]()
 
     @pl.loop(0, 2)
@@ -641,20 +660,35 @@
     def _(k):
         @pl.when(k == 2)
         def _():
+            ag_kv[5]()
             ag_o[3]()
             ag_m[2]()
-            ag_kv[5]()
 
         side(forward, 1 + 2 * k - 3 * lax.div(k, 2))
 
     ag_o[4]()
     ag_o[5]()
 
+    for n, k in enumerate(steps):
+        gates.got(R.gt.at[up(y, 4 - k)], 6 + n)
+    lower = lax.broadcasted_iota(jnp.int32, (16, 128), 1) < 64
+
+    def regroup(u, w):
+        return (
+            jnp.where(lower, u, pltpu.roll(w, 64, 1)),
+            jnp.where(lower, pltpu.roll(u, 64, 1), w),
+        )
+
+    for m in range(8):
+        u, w = (R.gt[q // 4, q % 4].astype(F32) for q in (2 * m, 2 * m + 1))
+        u, w = regroup(u, w)
+        R.gtn[:, m * 128 : (m + 1) * 128] = u.astype(BF)
+        R.gtn[:, 1024 + m * 128 : 1152 + m * 128] = w.astype(BF)
+
     @pl.loop(0, 2)
     def _(zi):
-        w = R.wo[:, :, :, :, :, 256:384].reshape(WIDTH, 128)
-        v = mm(R.xn[pl.ds(zi * 2, 2)].reshape(256, WIDTH), w)
-        R.gl[pl.ds(zi * 2, 2)] = v.reshape(2, 128, 128)
+        v = mm_tb(R.xn[pl.ds(zi * 2, 2)].reshape(256, WIDTH), R.gtn[...])
+        R.gl[pl.ds(zi * 2, 2)] = v.reshape(2, 128, 16)
 
     lanes = lax.broadcasted_iota(jnp.int32, (128, 128), 1)
 
@@ -682,7 +716,7 @@
 
         @pl.loop(0, 8, unroll=4)
         def _(n):
-            w = R.wo[lax.div(n, 4), lax.rem(n, 4), :, :, :, 0:256].reshape(256, 256)
+            w = R.wo[lax.div(n, 4), lax.rem(n, 4)].reshape(256, 256)
             cols = pl.ds(pl.multiple_of(n * 256, 256), 256)
             v = mm_tb(rows, w).astype(BF).reshape(2, 2, 64, 256)
             R.pb[cc, :, :, cols] = v[0]
@@ -711,6 +745,7 @@
     rs1.end()
     for g in (ex_a, ex_o, ex_m, ex_d):
         g[2]()
+    gates.end()
     ag_n.s0()
     ag_c[2]()
     ag_n.s1()
@@ -829,7 +864,7 @@
 
     @pl.loop(0, 2)
     def _(zi):
-        w = R.wo[:, :, :, :, :, 0:256].reshape(WIDTH, 256)
+        w = R.wo[...].reshape(WIDTH, 256)
         both = mm(R.nm[pl.ds(zi * 2, 2)].reshape(256, WIDTH), w)
         for ci in (0, 1):
             i, grad = zi * 2 + ci, both[ci * 128 : (ci + 1) * 128]
@@ -846,7 +881,6 @@
                 R.dox[zi, h, ci, :, 128:256] = three_parts(-delta, lanes)
             R.gsc[i, :, 512:640] = logits.astype(BF)
 
-    rs_d.t4()
     rs_f.s1()
 
     R.oacc[...] = jnp.zeros((2, 512, 256), F32)
@@ -903,6 +937,7 @@
         @pl.when(k == 1)
         def _():
             rs_k.t1(0)
+            rs_d.t4()
 
         @pl.when(k == 2)
         def _():
@@ -912,9 +947,6 @@
     rs_k.t2(0)
     rs_k.t2(1)
     rs_m.t3()
-    rs_d.t5()
-    tell(ring, R.free.at[2])
-    R.wm[:, y, x, :, :, 1536:2304] = R.ga[:, y, x, :, :, 0:768]
     near(backward, nothing)
     backward(own)
     rs_f.s3()
@@ -929,7 +961,11 @@
     tell(group, R.free.at[1])
     tw_o[0]()
 
+    rs_d.t5()
+    tell(ring, R.free.at[2])
+    R.wm[:, y, x, :, :, 1536:2304] = R.ga[:, y, x, :, :, 0:768]
     rs_k.t3()
+    rs_m.t4()
 
     R.dgh[...] = jnp.zeros((8, 128), F32)
 
@@ -944,7 +980,9 @@
             R.dgh[0:1, :] += dg
             R.gsc[i, :, h * 128 : (h + 1) * 128] = dv.astype(BF)
 
-    rs_m.t4()
+    rs_k.t4()
+
+    turned_gates = R.gsc[:, :, 512:640].reshape(512, 128).T[0:16]
 
     @pl.loop(0, 8, unroll=4)
     def _(n):
@@ -954,13 +992,23 @@
         t = turned(R.xn, n)
         g = mm(t, R.gsc[:, :, 0:256].reshape(512, 256))
         R.ga[at + (slice(256, 512),)] = g.astype(BF).reshape(4, 2, 32, 256)
-        g = mm(t, R.gsc[:, :, 512:640].reshape(512, 128))
-        R.ga[at + (slice(512, 640),)] = g.astype(BF).reshape(4, 2, 32, 128)
-
-    rs_e = scatter(R.ga, big, rings[2], slice(0, 640))
+        cols = pl.ds(pl.multiple_of(n * 256, 256), 256)
+        R.gtg[:, cols] = mm(turned_gates, R.xn[:, :, :, cols].reshape(512, 256))
+
+    for m in range(8):
+        u, w = (R.gtg[:, q + m * 128 : q + (m + 1) * 128] for q in (0, 1024))
+        u, w = regroup(u, w)
+        R.gg[m // 2, m % 2 * 2] = u.astype(BF)
+        R.gg[m // 2, m % 2 * 2 + 1] = w.astype(BF)
+    gates = Group(9, gates.base)
+    for n, k in enumerate(steps):
+        gates.go(R.gg.at[up(y, k)], R.gg_y.at[n], ydev[n], 6 + n)
+    rs_e = scatter(R.ga, big, rings[2], slice(0, 512))
     pl.semaphore_wait(R.free.at[2], 4)
-    rs_k.t4()
     rs_e.start()
+    rs_m.t5()
+    gb_m = give_back(R.wm, R.wlm, pairs[0])
+    gb_m[0]()
     rs_k.t5()
 
     @pl.loop(0, 4)
@@ -976,21 +1024,17 @@
     @pl.loop(0, 8, unroll=4)
     def _(n):
         g = mm(turned(R.xn, n), R.gsc[:, :, 256:512].reshape(512, 256))
-        R.ga[block(n) + (slice(640, 896),)] = g.astype(BF).reshape(4, 2, 32, 256)
-
-    rs_l = scatter(R.ga, small, rings[3], slice(640, 896), slice(0, 256), slice(0, 32))
+        R.ga[block(n) + (slice(512, 768),)] = g.astype(BF).reshape(4, 2, 32, 256)
+
+    rs_l = scatter(R.ga, small, rings[3], slice(512, 768), slice(0, 256), slice(0, 32))
     rs_l.start()
-    rs_m.t5()
-    gb_m = give_back(R.wm, R.wlm, pairs[0])
-    gb_m[0]()
 
     @pl.loop(0, 8, unroll=4)
     def _(n):
         at = block(n)
         v = mm_tb(R.gsc[:, :, 0:512].reshape(512, 512), R.wa[at].reshape(256, PROJ))
-        w = R.wo[at + (slice(256, 384),)].reshape(256, 128)
-        v = v + mm_tb(R.gsc[:, :, 512:640].reshape(512, 128), w)
         cols = pl.ds(pl.multiple_of(n * 256, 256), 256)
+        v = v + mm(R.gsc[:, :, 512:528].reshape(512, 16), R.gtn[:, cols])
         dg = jnp.sum(v * R.xn[:, :, :, cols].reshape(512, 256).astype(F32), axis=0, keepdims=True)
         R.dgs[0:1, cols] = dg / R.ag[:, cols]
         cols, v = spread(n, v)
@@ -1022,15 +1066,30 @@
 
     fin = add_up(0, group + zsib)
     rs_e.onward()
+    for n in range(3):
+        gates.got(R.gg_y.at[n], 6 + n)
+    v = R.gg[y].astype(F32)
+    for n in range(3):
+        v = v + R.gg_y[n].astype(F32)
+    R.gg[y] = v.astype(BF)
+    for n, k in enumerate(steps):
+        gates.go(R.gg.at[y, up(x, k)], R.gg_x.at[n], xdev[n], 3 + n)
     rs3.s1()
     rs_l.onward()
     rs3.s2()
     fin()
     fin = add_up(1, xdev)
     rs_e.t3()
-    fin()
-    fin = add_up(2, ydev)
     rs_l.t3()
+    for n in range(3):
+        gates.got(R.gg_x.at[n], 3 + n)
+    v = R.gg[y, x].astype(F32)
+    for n in range(3):
+        v = v + R.gg_x[n].astype(F32)
+    R.gt_out[me] = v.astype(BF)
+    for n, (_, d) in enumerate(near_group):
+        gates.go(R.gt_out.at[me], R.gt_out.at[me], d, n)
+    rs_e.t4()
     rs3.s3()
     tw_i = twin(R.ib)
 
@@ -1043,8 +1102,14 @@
 
     tw_i[0]()
     rs3.end()
-    rs_e.t4()
+    fin()
+    fin = add_up(2, ydev)
     rs_l.t4()
+    rs_e.t5()
+    rs_l.t5()
+    gb_a = give_back(R.ga, R.wl8, pairs[1])
+    gb_a[0]()
+
     def put(i, src, dst):
         cp = pltpu.make_async_copy(src, dst, R.put.at[i])
         cp.start()
@@ -1056,12 +1121,12 @@
     puts.append(put(1, R.ob, R.o_out))
     fin()
     puts.append(put(2, R.sums.at[3], R.o_gain))
-    rs_e.t5()
-    rs_l.t5()
-    gb_a = give_back(R.ga, R.wl8, pairs[1])
-    gb_a[0]()
     tw_i[1]()
     puts.append(put(3, R.ib, R.o_in))
+    for n, (i, _) in enumerate(near_group):
+        gates.got(R.gt_out.at[i], n)
+    gates.end()
+    puts.append(put(5, R.gt_out, R.o_gt))
     gb_a[1]()
     puts.append(put(4, R.wl8, R.o_fa))
     for cp in puts:
@@ -1084,6 +1149,7 @@
     ("o_gain", (40, 128), F32),
     ("o_fm", (4, 32, 2304), BF),
     ("o_fa", (4, 32, ATT), BF),
+    ("o_gt", (4, 16, 128), BF),
 ]
 RESULTS = [
     ((128, WIDTH), BF),
@@ -1103,11 +1169,20 @@
 ]
 SCRATCH = [
     ("wla", (4, 32, PROJ), BF),
-    ("wlo", (4, 32, 384), BF),
+    ("wlo", (4, 32, 256), BF),
     ("wl8", (4, 32, ATT), BF),
     ("wlm", (4, 32, 2304), BF),
     ("wa", (2, 4, 4, 2, 32, PROJ), BF),
-    ("wo", (2, 4, 4, 2, 32, 384), BF),
+    ("wo", (2, 4, 4, 2, 32, 256), BF),
+    ("gt_l", (4, 16, 128), BF),
+    ("gt_in", (4, 16, 128), BF),
+    ("gt", (4, 4, 16, 128), BF),
+    ("gtn", (16, WIDTH), BF),
+    ("gtg", (16, WIDTH), F32),
+    ("gg", (4, 4, 16, 128), BF),
+    ("gg_y", (3, 4, 16, 128), BF),
+    ("gg_x", (3, 16, 128), BF),
+    ("gt_out", (4, 16, 128), BF),
     ("ga", (2, 4, 4, 2, 32, ATT), BF),
     ("wm", (2, 4, 4, 2, 32, 2304), BF),
     ("kv", (2, 4, 4, 2, 128, 256), BF),
@@ -1118,7 +1193,7 @@
     ("sin", (4, 128, 128), F32),
     ("qraw", (4, 128, 256), F32),
     ("kraw", (4, 128, 128), F32),
-    ("gl", (4, 128, 128), F32),
+    ("gl", (4, 128, 16), F32),
     ("qx", (2, 2, 2, 128, 256), BF),
     ("dox", (2, 2, 2, 128, 256), BF),
     ("oacc", (2, 512, 256), F32),
@@ -1147,7 +1222,7 @@
     ("sums", (4, 40, 128), F32),
     ("came", (13, 40, 128), F32),
 ]
-COPIES = 175
+COPIES = 184
 
 
 def kernel(*refs):
@@ -1155,7 +1230,7 @@
     body(SimpleNamespace(**dict(zip(names, refs))))
 
 
-def finish(out, grad_in, gain, fm, fa, *to):
+def finish(out, grad_in, gain, fm, fa, gt, *to):
     to[0][...] = out[...].reshape(128, WIDTH)
     to[1][...] = grad_in[...].reshape(128, WIDTH)
     place = lax.axis_index("seq")
@@ -1164,20 +1239,19 @@
         to[at][...] = pltpu.roll(v, lax.rem(128 - lax.rem(place, 4) * 32, 128), 1)[:, 0:32]
     to[7][...] = gain[32:33, :]
     to[8][...] = gain[33:34, :]
-    gates = jnp.zeros((8, 32), F32)
+    ours = lax.div(place, 32) * 2 + lax.rem(place, 2)
     for i in range(4):
         wide = slice(i * 256, (i + 1) * 256)
         low = slice(i * 128, (i + 1) * 128)
         to[9][:, wide] = fa[i, :, 0:256].astype(F32)
         to[3][:, wide] = fa[i, :, 256:512].astype(F32)
-        to[4][:, low] = fa[i, :, 640:768].astype(F32)
-        to[5][:, low] = fa[i, :, 768:896].astype(F32)
-        pick = select(lambda r, q, i=i: (r == q + 2 * i) & (q < 2), (8, 128))
-        gates = gates + mm_tb(pick, fa[i, :, 512:640])
+        to[4][:, low] = fa[i, :, 512:640].astype(F32)
+        to[5][:, low] = fa[i, :, 640:768].astype(F32)
+        tile = pltpu.roll(gt[i].astype(F32), lax.rem(128 - ours * 32, 128), 1)
+        to[6][2 * i : 2 * i + 2, :] = tile[0:2, 0:32]
         for k in range(3):
             cols = slice(k * 768, (k + 1) * 768)
             to[11 + k][:, i * 768 : (i + 1) * 768] = fm[i, :, cols].astype(F32)
-    to[6][...] = gates
 
 
 def rope_tables():
@@ -1212,7 +1286,7 @@
         out_specs=[pl.BlockSpec(memory_space=pl.ANY)] * len(OUTPUTS),
         scratch_shapes=[pltpu.VMEM(shape, kind) for _, shape, kind in SCRATCH]
         + [pltpu.SemaphoreType.DMA((COPIES,)), pltpu.SemaphoreType.DMA((COPIES,))]
-        + [pltpu.SemaphoreType.REGULAR((3,)), pltpu.SemaphoreType.DMA((5,))],
+        + [pltpu.SemaphoreType.REGULAR((3,)), pltpu.SemaphoreType.DMA((6,))],
         compiler_params=pltpu.CompilerParams(
             collective_id=0, has_side_effects=True, vmem_limit_bytes=63 * 2**20
         ),

time: 213 us -> 210 us (0.986)
  Pallas kernels: 213 us -> 209 us
    pallas_call x1, Pallas kernels: 210 us -> 206 us  [per_device(): pl.pallas_call(kernel, out_shape=[jax.ShapeDtypeStruct(shape, kind) for _...]
where the time goes in v1:
time: 210 us
  Pallas kernels  209 us (100%)
    pallas_call x1, Pallas kernels, per_device(): pl.pallas_call(kernel, out_shape=[jax.ShapeDtypeStruct(shape, kind) for _...  206 us

profile of v1, /device:TPU:1, one launch (start us, length us, event | category | flops | bytes accessed | tf_op | source)
XLA Modules:
  0.0 210.0 jit_solution(5768884883681399378)
XLA Ops:
  0.7 206.2 %block.1 = (bf16[2,64,2048]{2,1,0:T(8,128)(2,1)}, bf16[2,64,2048]{2,1,0:T(8,128)(2,1)}, f32[40,128]{1,0:T(8,128)}, bf16[4,32,2304]{2,1,0:T(8,128)(2,1)}, bf16[4,...) custom-call(bf16[128,2048]{1,0:T(8,128)(2,1)} %refs_0_.1, bf16[128,2048]{1,0:T(8,128)(2,1)} %refs_1_.1, ...), custom_call_target="tpu_custom_call" | custom-call | tf_op jit(solution)/shard_map/block/pallas_call | solution.py:1282
  206.9 3.0 %results.1 = (bf16[128,2048]{1,0:T(8,128)(2,1)}, bf16[128,2048]{1,0:T(8,128)(2,1)}, f32[1,32]{1,0:T(1,128)}, f32[32,1024]{1,0:T(8,128)}, f32[32,512]{1,0:T(8,128...) custom-call(bf16[2,64,2048]{2,1,0:T(8,128)(2,1)} %get-tuple-element., ...), custom_call_target="tpu_custom_call" | custom-call | tf_op jit(solution)/shard_map/results/pallas_call | solution.py:1311

commit v2 on v1

--- a/solution.py
+++ b/solution.py
@@ -96,21 +96,26 @@
     for d in greet:
         pl.semaphore_signal(barrier, inc=1, device_id=d, device_id_type=MESH)
 
-    count = [0]
+    count, sends, first_send = [0], [0], {}
+
+    def take(counter, k):
+        counter[0] += k
+        return counter[0] - k
 
     def ids(k):
-        count[0] += k
-        return count[0] - k
+        return take(count, k)
 
     class Group:
-        def __init__(self, k, base=None):
-            self.base, self.sent = ids(k) if base is None else base, []
+        def __init__(self, k, base=None, whole=None):
+            self.base, self.whole, self.sent = ids(k) if base is None else base, whole, []
+            if self.base not in first_send:
+                first_send[self.base] = take(sends, 1 if whole else k)
 
         def copy(self, src, dst, d, i):
-            i += self.base
+            out = first_send[self.base] + (0 if self.whole else i)
             return pltpu.make_async_remote_copy(
-                src_ref=src, dst_ref=dst, send_sem=R.send.at[i], recv_sem=R.recv.at[i],
-                device_id=d, device_id_type=MESH,
+                src_ref=src, dst_ref=dst, send_sem=R.send.at[out],
+                recv_sem=R.recv.at[self.base + i], device_id=d, device_id_type=MESH,
             )
 
         def run(self, ends, d, i):
@@ -124,8 +129,12 @@
             self.copy(ref, ref, sib, i).wait_recv()
 
         def end(self):
-            for cp in self.sent:
-                cp().wait_send()
+            if self.whole:
+                ref = self.whole()
+                self.copy(ref, ref, sib, 0).wait_send()
+            else:
+                for cp in self.sent:
+                    cp().wait_send()
 
     def exchange(buf, wl, base, cs=ALL):
         g = Group(3, base)
@@ -161,29 +170,31 @@
         return start, wait, g.end
 
     a_y = SimpleNamespace(
-        full=lambda p: (0, p), half=lambda p, h: (0, p, ALL, h), elem=lambda p, k, h: (0, p, k, h),
+        three=(0, slice(0, 3)), half=lambda p, h: (0, p, ALL, h), elem=lambda p, k, h: (0, p, k, h),
         k=4, pos=y, dev=ydev,
     )
     a_x = SimpleNamespace(
-        full=lambda p: (0, y, p), half=lambda p, h: (0, y, p, h), elem=lambda p, k, h: (0, y, p, h),
+        three=(0, y, slice(0, 3)), half=lambda p, h: (0, y, p, h), elem=lambda p, k, h: (0, y, p, h),
         k=1, pos=x, dev=xdev,
     )
     b_x = SimpleNamespace(
-        full=lambda p: (1, ALL, p), half=lambda p, h: (1, ALL, p, h), elem=lambda p, k, h: (1, k, p, h),
+        three=(1, ALL, slice(0, 3)), half=lambda p, h: (1, ALL, p, h), elem=lambda p, k, h: (1, k, p, h),
         k=4, pos=x, dev=xdev,
     )
     b_y = SimpleNamespace(
-        full=lambda p: (1, p, x), half=lambda p, h: (1, p, x, h), elem=lambda p, k, h: (1, p, x, h),
+        three=(1, slice(0, 3), x), half=lambda p, h: (1, p, x, h), elem=lambda p, k, h: (1, p, x, h),
         k=1, pos=y, dev=ydev,
     )
 
     def gather_ring(buf, a, cs, base):
-        g, p = Group(6, base), a.pos
+        def cut(at):
+            return buf.at[at if cs is None else at + (ALL,) * (5 - len(at)) + (cs,)]
+
+        g, p = Group(6, base, lambda: cut(a.three)), a.pos
         left, right, across = up(p, 3), up(p, 1), up(p, 2)
 
         def half(q, h):
-            at = a.half(q, h)
-            return buf.at[at if cs is None else at + (ALL,) * (5 - len(at)) + (cs,)]
+            return cut(a.half(q, h))
 
         def s1():
             for i, (h, d) in enumerate(((0, 0), (1, 1), (1, 0), (0, 1))):
@@ -240,13 +251,15 @@
         return t1, t2, t3, t4, t5, t6
 
     def reduce_ring(buf, a, r2, r1, cs, bs, rows, base):
-        g, p, k = Group(6, base), a.pos, a.k
+        def cut(at):
+            return buf.at[at + (ALL,) * (5 - len(at)) + (cs,)]
+
+        g, p, k = Group(6, base, lambda: cut(a.three)), a.pos, a.k
         first = ALL if k == 4 else 0
         across, beside = up(p, 2), (up(p, 1), up(p, 3))
 
         def half(q, h):
-            at = a.half(q, h)
-            return buf.at[at + (ALL,) * (5 - len(at)) + (cs,)]
+            return cut(a.half(q, h))
 
         def elem(q, n, h):
             return a.elem(q, n, h) + (ALL, cs)
@@ -479,7 +492,7 @@
         R.wla[i, :, 0:256] = R.qw[:, i * 256 : (i + 1) * 256]
         R.wla[i, :, 256:384] = R.kw[:, i * 128 : (i + 1) * 128]
         R.wla[i, :, 384:512] = R.vw[:, i * 128 : (i + 1) * 128]
-    pairs, rings = [ids(3) for _ in range(4)], [ids(24) for _ in range(5)]
+    pairs, rings = [ids(3) for _ in range(4)], [ids(24) for _ in range(4)]
     ex_a = exchange(R.wa, R.wla, pairs[0])
     ex_o = exchange(R.wo, R.wlo, pairs[1])
     ex_m = exchange(R.wm, R.wlm, pairs[2], slice(0, 1536))
@@ -489,7 +502,7 @@
     ag_d = gather(R.wm, rings[3], slice(1536, 2304))
     ag_x = gather_blocks(R.xn)
     ag_c = gather_blocks(R.cot)
-    ag_kv = gather(R.kv, rings[4])
+    ag_kv = gather(R.kv, rings[0])
 
     pl.semaphore_wait(barrier, len(greet))
     ex_a[0]()
@@ -779,8 +792,8 @@
         return ref[:, :, :, cols].reshape(512, 256).T
 
     big = (R.m_r2, R.m_r1, R.m_q2, R.m_q1)
-    rs_d = scatter(R.ga, big, rings[0], slice(0, 768))
-    rs_m = scatter(R.wm, big, rings[1], slice(0, 1536), slice(768, 2304))
+    rs_d = scatter(R.ga, big, rings[1], slice(0, 768))
+    rs_m = scatter(R.wm, big, rings[2], slice(0, 1536), slice(768, 2304))
 
     @pl.loop(0, 8, unroll=4)
     def _(n):
@@ -820,6 +833,7 @@
     rs2.s1()
     rs_d.onward()
     pl.loop(4, 8, unroll=4)(feed_weights)
+    rs_m.start()
     rs2.s2()
 
     def tell(devices, sem):
@@ -831,7 +845,6 @@
     ag_n.end()
     tell(group, R.free.at[0])
     ag_h = gather_rows(R.nm)
-    rs_m.start()
 
     @pl.loop(0, 8, unroll=4)
     def _(n):
@@ -924,7 +937,7 @@
         R.kv[at] = jnp.zeros((2, 128, 256), BF)
 
     small = (R.k_r2, R.k_r1, R.k_q2, R.k_q1)
-    rs_k = scatter(R.kv, small, rings[4], slice(0, 256))
+    rs_k = scatter(R.kv, small, rings[0], slice(0, 256))
 
     @pl.loop(0, 3)
     def _(k):
@@ -1003,7 +1016,7 @@
     gates = Group(9, gates.base)
     for n, k in enumerate(steps):
         gates.go(R.gg.at[up(y, k)], R.gg_y.at[n], ydev[n], 6 + n)
-    rs_e = scatter(R.ga, big, rings[2], slice(0, 512))
+    rs_e = scatter(R.ga, big, rings[3], slice(0, 512))
     pl.semaphore_wait(R.free.at[2], 4)
     rs_e.start()
     rs_m.t5()
@@ -1026,7 +1039,7 @@
         g = mm(turned(R.xn, n), R.gsc[:, :, 256:512].reshape(512, 256))
         R.ga[block(n) + (slice(512, 768),)] = g.astype(BF).reshape(4, 2, 32, 256)
 
-    rs_l = scatter(R.ga, small, rings[3], slice(512, 768), slice(0, 256), slice(0, 32))
+    rs_l = scatter(R.ga, small, rings[1], slice(512, 768), slice(0, 256), slice(0, 32))
     rs_l.start()
 
     @pl.loop(0, 8, unroll=4)
@@ -1135,7 +1148,7 @@
     ag_h.end()
     gb_m[2]()
     gb_a[2]()
-    assert count[0] == COPIES, count
+    assert (count[0], sends[0]) == (COPIES, SENDS), (count, sends)
 
 
 INPUTS = [
@@ -1222,7 +1235,7 @@
     ("sums", (4, 40, 128), F32),
     ("came", (13, 40, 128), F32),
 ]
-COPIES = 184
+COPIES, SENDS = 160, 80
 
 
 def kernel(*refs):
@@ -1285,7 +1298,7 @@
         in_specs=[vmem] * len(INPUTS),
         out_specs=[pl.BlockSpec(memory_space=pl.ANY)] * len(OUTPUTS),
         scratch_shapes=[pltpu.VMEM(shape, kind) for _, shape, kind in SCRATCH]
-        + [pltpu.SemaphoreType.DMA((COPIES,)), pltpu.SemaphoreType.DMA((COPIES,))]
+        + [pltpu.SemaphoreType.DMA((SENDS,)), pltpu.SemaphoreType.DMA((COPIES,))]
         + [pltpu.SemaphoreType.REGULAR((3,)), pltpu.SemaphoreType.DMA((6,))],
         compiler_params=pltpu.CompilerParams(
             collective_id=0, has_side_effects=True, vmem_limit_bytes=63 * 2**20

time: 210 us -> 209 us (level)
  no operation moved by 1% of the time
where the time goes in v2:
time: 209 us; the launch traced here: 208 us
  Pallas kernels  208 us (100%)
    pallas_call x1, Pallas kernels, per_device(): pl.pallas_call(kernel, out_shape=[jax.ShapeDtypeStruct(shape, kind) for _...  205 us

profile of v2, /device:TPU:1, one launch (start us, length us, event | category | flops | bytes accessed | tf_op | source)
XLA Modules:
  0.0 208.4 jit_solution(15024540939368819677)
XLA Ops:
  0.7 204.6 %block.1 = (bf16[2,64,2048]{2,1,0:T(8,128)(2,1)}, bf16[2,64,2048]{2,1,0:T(8,128)(2,1)}, f32[40,128]{1,0:T(8,128)}, bf16[4,32,2304]{2,1,0:T(8,128)(2,1)}, bf16[4,...) custom-call(bf16[128,2048]{1,0:T(8,128)(2,1)} %refs_0_.1, bf16[128,2048]{1,0:T(8,128)(2,1)} %refs_1_.1, ...), custom_call_target="tpu_custom_call" | custom-call | tf_op jit(solution)/shard_map/block/pallas_call | solution.py:1295
  205.2 3.0 %results.1 = (bf16[128,2048]{1,0:T(8,128)(2,1)}, bf16[128,2048]{1,0:T(8,128)(2,1)}, f32[1,32]{1,0:T(1,128)}, f32[32,1024]{1,0:T(8,128)}, f32[32,512]{1,0:T(8,128...) custom-call(bf16[2,64,2048]{2,1,0:T(8,128)(2,1)} %get-tuple-element., ...), custom_call_target="tpu_custom_call" | custom-call | tf_op jit(solution)/shard_map/results/pallas_call | solution.py:1324

commit v3 on v2

--- a/solution.py
+++ b/solution.py
@@ -894,7 +894,6 @@
                 R.dox[zi, h, ci, :, 128:256] = three_parts(-delta, lanes)
             R.gsc[i, :, 512:640] = logits.astype(BF)
 
-    rs_f.s1()
 
     R.oacc[...] = jnp.zeros((2, 512, 256), F32)
     row_t = lax.broadcasted_iota(jnp.int32, (256, 512), 1)
@@ -956,12 +955,14 @@
         def _():
             rs_k.t1(1)
 
-    rs_f.s2()
+    rs_f.s1()
     rs_k.t2(0)
     rs_k.t2(1)
     rs_m.t3()
     near(backward, nothing)
     backward(own)
+    rs_f.s2()
+    rs_d.t5()
     rs_f.s3()
     tw_o = twin(R.ob)
 
@@ -974,7 +975,6 @@
     tell(group, R.free.at[1])
     tw_o[0]()
 
-    rs_d.t5()
     tell(ring, R.free.at[2])
     R.wm[:, y, x, :, :, 1536:2304] = R.ga[:, y, x, :, :, 0:768]
     rs_k.t3()

time: 209 us -> 209 us (level)
  no operation moved by 1% of the time
where the time goes in v3:
time: 209 us; the launch traced here: 208 us
  Pallas kernels  208 us (100%)
    pallas_call x1, Pallas kernels, per_device(): pl.pallas_call(kernel, out_shape=[jax.ShapeDtypeStruct(shape, kind) for _...  205 us

profile of v3, /device:TPU:1, one launch (start us, length us, event | category | flops | bytes accessed | tf_op | source)
XLA Modules:
  0.0 208.4 jit_solution(16838290351549730219)
XLA Ops:
  0.7 204.6 %block.1 = (bf16[2,64,2048]{2,1,0:T(8,128)(2,1)}, bf16[2,64,2048]{2,1,0:T(8,128)(2,1)}, f32[40,128]{1,0:T(8,128)}, bf16[4,32,2304]{2,1,0:T(8,128)(2,1)}, bf16[4,...) custom-call(bf16[128,2048]{1,0:T(8,128)(2,1)} %refs_0_.1, bf16[128,2048]{1,0:T(8,128)(2,1)} %refs_1_.1, ...), custom_call_target="tpu_custom_call" | custom-call | tf_op jit(solution)/shard_map/block/pallas_call | solution.py:1295
  205.2 3.0 %results.1 = (bf16[128,2048]{1,0:T(8,128)(2,1)}, bf16[128,2048]{1,0:T(8,128)(2,1)}, f32[1,32]{1,0:T(1,128)}, f32[32,1024]{1,0:T(8,128)}, f32[32,512]{1,0:T(8,128...) custom-call(bf16[2,64,2048]{2,1,0:T(8,128)(2,1)} %get-tuple-element., ...), custom_call_target="tpu_custom_call" | custom-call | tf_op jit(solution)/shard_map/results/pallas_call | solution.py:1324
